TPU v7x, 512 devices: a whole 4x4x16 slice. The times are simulated.
512 devices in a mesh: blk: 16 (over y, x_hi, core), dom: 32 (over z, x_lo).
Axes of the slice: x: 4 (x_hi: 2, x_lo: 2; x = x_hi * 2 + x_lo), y: 4, z: 16, core: 2. Of those that a mesh axis runs over, the one named last changes fastest.
Arguments:
- hidden_values: bfloat16 [65536, 256], P(('blk', 'dom')), may hold values from -6 to 6
- node_scale: float32 [65536], P(('blk', 'dom')), may hold values from 0.25 to 2
- node_weight: int32 [65536], P(('blk', 'dom')), may hold values from 8 to 24
- weight: bfloat16 [256, 256], replicated, may hold values from -0.375 to 0.375
- cotangent: bfloat16 [65536, 256], P(('blk', 'dom')), may hold values from -6 to 6
- block_rows: int32 [16, 32, 96], P('blk', 'dom'), may hold values from 0 to 31
- block_cols: int32 [16, 32, 96], P('blk', 'dom'), may hold values from 0 to 15
- block_count: int32 [16, 32], P('blk', 'dom'), may hold values from 1 to 96, as said below
- edge_counts: bfloat16 [16, 32, 96, 128, 128], P('blk', 'dom'), may hold values from 0 to 3, as said below
Outputs:
- activated: bfloat16 [65536, 256], P(('blk', 'dom'))
- grad_hidden: bfloat16 [65536, 256], P(('blk', 'dom'))
Inputs may be any that keep to these rules, and one draw needn't show every extreme that they name: The first block_count[b, d] slots of a device hold its blocks and the others are unused; some device uses all 96 slots. `edge_counts`: whole numbers of edges; most entries of a block are zero.
All inputs are finite; a program needn't handle non-finite values.
Results may differ from a plain program's by a relative error of at most 0.028.
Values may be sent and summed in bfloat16 or wider, within the bound.
No kernel may reach another device: no remote copies, remote signals or barrier semaphores. Data moves between devices by JAX's collectives and lax.ppermute only.
A program may use at most 64 MiB of HBM per device.

v0:
```python
import jax
import jax.numpy as jnp
from jax import lax
from jax.sharding import PartitionSpec as P

HID = 256
BSZ = 128
QDEN = 192
slot_group = 16


def add_group(running, offset, edge_local, live_count, pick_index, place_index, source, pattern):
    chosen = lax.dynamic_slice_in_dim(edge_local, offset, slot_group, 0)
    slot_ids = offset + jnp.arange(slot_group, dtype=jnp.int32)
    chosen = jnp.where((slot_ids < live_count)[:, None, None], chosen, jnp.zeros_like(chosen))
    pick_rows = lax.dynamic_slice_in_dim(pick_index, offset, slot_group, 0)
    places = lax.dynamic_slice_in_dim(place_index, offset, slot_group, 0)
    tile_rows = jnp.take(source, pick_rows, axis=0)
    contrib = jnp.einsum(pattern, chosen, tile_rows, preferred_element_type=jnp.float32)
    return running.at[places].add(contrib)


def accumulate(
    running, group_turns, edge_local, live_count, pick_index, place_index, source, pattern
):

    def one_group(group_number, current):
        return add_group(
            current,
            group_number * slot_group,
            edge_local,
            live_count,
            pick_index,
            place_index,
            source,
            pattern,
        )

    return lax.fori_loop(0, group_turns, one_group, running)


def slope_of(preact):
    sigmoid_pre = jax.nn.sigmoid(preact)
    return sigmoid_pre * (1.0 + preact * (1.0 - sigmoid_pre))


def per_device(
    hidden_values,
    node_scale,
    node_weight,
    weight,
    cotangent,
    block_rows,
    block_cols,
    block_count,
    edge_counts,
):
    own_rows = hidden_values.shape[0]
    node_norm = node_weight.astype(jnp.float32) / QDEN
    scaled = (hidden_values.astype(jnp.float32) * (node_scale * node_norm)[:, None]).astype(
        jnp.bfloat16
    )
    gathered = lax.all_gather(scaled, "blk", axis=0, tiled=True)
    column_tiles = gathered.reshape(-1, BSZ, HID)
    edge_local = edge_counts[0, 0]
    rows_local = block_rows[0, 0]
    cols_local = block_cols[0, 0]
    live_count = block_count[0, 0]
    slot_total = edge_local.shape[0]
    group_turns = slot_total // slot_group
    row_blocks = lax.axis_size("dom") * (own_rows // BSZ)
    forward_sums = accumulate(
        jnp.zeros((row_blocks, BSZ, HID), jnp.float32),
        group_turns,
        edge_local,
        live_count,
        cols_local,
        rows_local,
        column_tiles,
        "kji,kjh->kih",
    )
    forward_flat = forward_sums.reshape(row_blocks * BSZ, HID)
    summed = lax.psum_scatter(
        forward_flat.astype(jnp.bfloat16), "dom", scatter_dimension=0, tiled=True
    ).astype(jnp.float32)
    aggregated = (summed * node_norm[:, None]).astype(jnp.bfloat16)
    preact = jnp.dot(aggregated, weight, preferred_element_type=jnp.float32)
    activated = jax.nn.silu(preact).astype(jnp.bfloat16)
    dpre = (cotangent.astype(jnp.float32) * slope_of(preact)).astype(jnp.bfloat16)
    back_own = (
        jnp.dot(dpre, weight.T, preferred_element_type=jnp.float32) * node_norm[:, None]
    ).astype(jnp.bfloat16)
    back_all = lax.all_gather(back_own, "dom", axis=0, tiled=True)
    row_tiles = back_all.reshape(-1, BSZ, HID)
    column_blocks = column_tiles.shape[0]
    backward_sums = accumulate(
        jnp.zeros((column_blocks, BSZ, HID), jnp.float32),
        group_turns,
        edge_local,
        live_count,
        rows_local,
        cols_local,
        row_tiles,
        "kji,kih->kjh",
    )
    column_sums = lax.psum_scatter(
        backward_sums.reshape(column_blocks * BSZ, HID).astype(jnp.bfloat16),
        "blk",
        scatter_dimension=0,
        tiled=True,
    ).astype(jnp.float32)
    grad_hidden = (column_sums * node_norm[:, None]).astype(jnp.bfloat16)
    return (activated, grad_hidden)


def solution(mesh):
    return jax.shard_map(
        per_device,
        mesh=mesh,
        in_specs=(
            P(("blk", "dom"), None),
            P(("blk", "dom")),
            P(("blk", "dom")),
            P(),
            P(("blk", "dom"), None),
            P("blk", "dom", None),
            P("blk", "dom", None),
            P("blk", "dom"),
            P("blk", "dom", None, None, None),
        ),
        out_specs=(P(("blk", "dom"), None), P(("blk", "dom"), None)),
        check_vma=False,
    )
```

profile of v0, /device:TPU:32, one launch (start us, length us, event | category | flops | bytes accessed | tf_op | source)
XLA Modules:
  0.0 574.5 jit_solution(5993749015452363039)
XLA Ops:
  7.9 1.6 multiply_convert_fusion.4
  9.6 66.7 %all-gather.3.cloned.1.call-done = bf16[2048,256]{1,0:T(8,128)(2,1)} async-done(((bf16[128,256]{1,0:T(8,128)(2,1)}), bf16[2048,256]{1,0:T(8,128)(2,1)}) %all-gather.3.cloned.1.call-update) | async-done | bytes 1048592 | tf_op jit(solution)/shard_map/all_gather | solution.py:63
  76.3 2.4 broadcast_in_dim.111
  78.7 64.9 %while.26 = (s32[]{:T(128)}, f32[32,128,256]{2,1,0:T(8,128)}, s32[96]{0:T(128)S(1)}, s32[]{:T(128)}, bf16[96,128,128]{2,1,0:T(8,128)(2,1)}, /*index=5*/s32[96]{0...) while((s32[]{:T(128)}, f32[32,128,256]{2,1,0:T(8,128)}, ...), condition=%wide.region_2.3_spmd, body=%wide.region_0.2_spmd.sunk | while | flops 135529648 | bytes 14160559 | solution.py:39
  79.5 1.8 gather_fusion
  83.4 1.5 fusion.36
  85.1 4.4 scatter_fusion
  90.2 1.8 gather_fusion
  94.2 1.5 fusion.36
  95.8 4.4 scatter_fusion
  100.9 1.8 gather_fusion
  104.9 1.5 fusion.36
  106.5 4.6 scatter_fusion
  111.8 1.8 gather_fusion
  115.8 1.5 fusion.36
  117.5 4.5 scatter_fusion
  122.7 1.8 gather_fusion
  126.7 1.5 fusion.36
  128.3 4.5 scatter_fusion
  133.6 1.8 gather_fusion
  139.2 4.4 scatter_fusion
  143.6 3.8 convert_element_type.48
  147.5 135.7 %reduce-scatter.3.cloned.1.call-done = bf16[128,256]{1,0:T(8,128)(2,1)} async-done(((bf16[4096,256]{1,0:T(8,128)(2,1)}), bf16[128,256]{1,0:T(8,128)(2,1)}) %reduce-scatter.3.cloned.1.call-update) | async-done | bytes 65552 | tf_op jit(solution)/shard_map/reduce_scatter | solution.py:83
  283.2 1.7 multiply_convert_fusion.2
  285.8 132.6 %all-gather.5.cloned.1.call-done = bf16[4096,256]{1,0:T(8,128)(2,1)} async-done(((bf16[128,256]{1,0:T(8,128)(2,1)}), bf16[4096,256]{1,0:T(8,128)(2,1)}) %all-gather.5.cloned.1.call-update) | async-done | bytes 2097168 | tf_op jit(solution)/shard_map/all_gather | solution.py:93
  418.4 1.5 broadcast_in_dim.112
  419.9 53.5 %while.27 = (s32[]{:T(128)}, f32[16,128,256]{2,1,0:T(8,128)}, s32[96]{0:T(128)S(1)}, s32[]{:T(128)}, bf16[96,128,128]{2,1,0:T(8,128)(2,1)}, /*index=5*/s32[96]{0...) while((s32[]{:T(128)}, f32[16,128,256]{2,1,0:T(8,128)}, ...), condition=%wide.region_6.7_spmd, body=%wide.region_4.6_spmd.sunk | while | flops 135529648 | bytes 12063407 | solution.py:39
  420.7 2.2 gather_fusion.1
  422.9 1.5 fusion.39
  424.5 4.3 scatter_fusion.1
  429.6 2.2 gather_fusion.1
  431.8 1.5 fusion.39
  433.4 4.3 scatter_fusion.1
  438.5 2.2 gather_fusion.1
  440.7 1.5 fusion.39
  442.3 4.4 scatter_fusion.1
  447.4 2.2 gather_fusion.1
  449.6 1.5 fusion.39
  451.3 4.4 scatter_fusion.1
  456.4 2.2 gather_fusion.1
  458.6 1.5 fusion.39
  460.2 4.3 scatter_fusion.1
  465.3 2.2 gather_fusion.1
  467.5 1.5 fusion.39
  469.1 4.4 scatter_fusion.1
  473.5 2.7 convert_element_type.56
  476.2 90.2 %reduce-scatter.5.cloned.1.call-done = bf16[128,256]{1,0:T(8,128)(2,1)} async-done(((bf16[2048,256]{1,0:T(8,128)(2,1)}), bf16[128,256]{1,0:T(8,128)(2,1)}) %reduce-scatter.5.cloned.1.call-update) | async-done | bytes 65552 | tf_op jit(solution)/shard_map/reduce_scatter | solution.py:106
  566.4 1.6 multiply_convert_fusion
  (67 shorter events, 25.9 us)
Async XLA Ops:
  7.2 276.0 %copy-start = (bf16[256,256]{1,0:T(8,128)(2,1)S(1)}, bf16[256,256]{1,0:T(8,128)(2,1)}, u32[]{:S(2)}) copy-start(bf16[256,256]{1,0:T(8,128)(2,1)} %param.16) | copy-start | bytes 393220
  7.2 69.1 %all-gather.3.cloned.1.call-start = ((), (), s32[]{:S(2)}) async-start(), calls=%async_computation.2 | async-start | bytes 1114112 | tf_op jit(solution)/shard_map/all_gather | solution.py:63
  9.5 273.7 %reduce-scatter.3.cloned.1.call-start = ((), (), s32[]{:S(2)}) async-start(), calls=%async_computation.3 | async-start | bytes 2162688 | tf_op jit(solution)/shard_map/reduce_scatter | solution.py:83
  76.3 2.4 copy-start.1
  76.3 2.4 copy-start.2
  147.5 137.5 %copy-start.3 = (bf16[128,256]{1,0:T(8,128)(2,1)S(1)}, bf16[128,256]{1,0:T(8,128)(2,1)}, u32[]{:S(2)}) copy-start(bf16[128,256]{1,0:T(8,128)(2,1)} %param.17) | copy-start | bytes 196612
  147.5 270.9 %all-gather.5.cloned.1.call-start = ((), (), s32[]{:S(2)}) async-start(), calls=%async_computation.4 | async-start | bytes 2162688 | tf_op jit(solution)/shard_map/all_gather | solution.py:93
  285.8 280.7 %reduce-scatter.5.cloned.1.call-start = ((), (), s32[]{:S(2)}) async-start(), calls=%async_computation.5 | async-start | bytes 1114112 | tf_op jit(solution)/shard_map/reduce_scatter | solution.py:106
Sparse Core Ops, SparseCore 0:
  11.9 64.2 all-gather.2
  147.6 135.5 reduce-scatter.2
  286.1 132.2 all-gather.4
  476.3 90.0 reduce-scatter.4
where the time goes:
time: 577 us; the launch traced here: 575 us
  waiting for transfers between devices  425 us (74%)
  other arithmetic  73 us (13%)
  local copies, waits for them, and re-layouts  41.1 us (7%)
  matrix products  21 us (4%)
  between operations  13.8 us (2%)
    reduce_scatter x1, waiting for transfers between devices, per_device(): lax.psum_scatter(forward_flat.astype(jnp.bfloat16), 'dom', scatter_dimens...  136 us
    all_gather x1, waiting for transfers between devices, per_device(): back_all = lax.all_gather(back_own, 'dom', axis=0, tiled=True)  133 us
    reduce_scatter x1, waiting for transfers between devices, per_device(): lax.psum_scatter(backward_sums.reshape(column_blocks * BSZ, HID).astype(j...  90.2 us
    all_gather x1, waiting for transfers between devices, per_device(): gathered = lax.all_gather(scaled, 'blk', axis=0, tiled=True)  66.7 us
    scatter-add x12, other arithmetic, add_group(): return running.at[places].add(contrib)  52.9 us
    gather x12, local copies, waits for them, and re-layouts, add_group(): tile_rows = jnp.take(source, pick_rows, axis=0)  24.3 us
    dot_general x12, matrix products, add_group(): jnp.einsum(pattern, chosen, tile_rows, preferred_element_type=jnp.float32)  18.5 us
    dynamic_slice x12, local copies, waits for them, and re-layouts, add_group(): chosen = lax.dynamic_slice_in_dim(edge_local, offset, slot_group, 0)  12.8 us
  transfers between devices with their start and end apart: 4, of which 4 were waited for; matrix products, arithmetic and copies ran while one was open for 0% of the time, Pallas kernels for 0%

commit v1 on v0

--- a/solution.py
+++ b/solution.py
@@ -60,7 +60,8 @@
     scaled = (hidden_values.astype(jnp.float32) * (node_scale * node_norm)[:, None]).astype(
         jnp.bfloat16
     )
-    gathered = lax.all_gather(scaled, "blk", axis=0, tiled=True)
+    repeated = jnp.stack([scaled] * lax.axis_size("blk"))
+    gathered = jnp.concatenate(lax.all_to_all(repeated, "blk", 0, 0), axis=0)
     column_tiles = gathered.reshape(-1, BSZ, HID)
     edge_local = edge_counts[0, 0]
     rows_local = block_rows[0, 0]

time: 577 us -> 536 us (0.929)
  waiting for transfers between devices: 425 us -> 377 us
  starting transfers between devices: 0.16 us -> 7.21 us
    all_gather x1 -> x0, waiting for transfers between devices: 66.7 us -> none  [per_device(): gathered = lax.all_gather(scaled, 'blk', axis=0, tiled=True)]
    all_to_all x0 -> x1, waiting for transfers between devices: none -> 18 us  [per_device(): gathered = jnp.concatenate(lax.all_to_all(repeated, 'blk', 0, 0), axis=0)]
    all_to_all x0 -> x1, starting transfers between devices: none -> 7.09 us  [per_device(): gathered = jnp.concatenate(lax.all_to_all(repeated, 'blk', 0, 0), axis=0)]
where the time goes in v1:
time: 536 us; the launch traced here: 534 us
  waiting for transfers between devices  377 us (70%)
  other arithmetic  72.2 us (13%)
  local copies, waits for them, and re-layouts  42 us (8%)
  matrix products  21 us (4%)
  between operations  13.8 us (3%)
  starting transfers between devices  7.21 us (1%)
    reduce_scatter x1, waiting for transfers between devices, per_device(): lax.psum_scatter(forward_flat.astype(jnp.bfloat16), 'dom', scatter_dimens...  136 us
    all_gather x1, waiting for transfers between devices, per_device(): back_all = lax.all_gather(back_own, 'dom', axis=0, tiled=True)  133 us
    reduce_scatter x1, waiting for transfers between devices, per_device(): lax.psum_scatter(backward_sums.reshape(column_blocks * BSZ, HID).astype(j...  90.3 us
    scatter-add x12, other arithmetic, add_group(): return running.at[places].add(contrib)  52.8 us
    gather x12, local copies, waits for them, and re-layouts, add_group(): tile_rows = jnp.take(source, pick_rows, axis=0)  24.3 us
    dot_general x12, matrix products, add_group(): jnp.einsum(pattern, chosen, tile_rows, preferred_element_type=jnp.float32)  18.5 us
    all_to_all x1, waiting for transfers between devices, per_device(): gathered = jnp.concatenate(lax.all_to_all(repeated, 'blk', 0, 0), axis=0)  18 us
    dynamic_slice x12, local copies, waits for them, and re-layouts, add_group(): chosen = lax.dynamic_slice_in_dim(edge_local, offset, slot_group, 0)  12.7 us
  transfers between devices with their start and end apart: 4, of which 4 were waited for; matrix products, arithmetic and copies ran while one was open for 0% of the time, Pallas kernels for 0%

profile of v1, /device:TPU:32, one launch (start us, length us, event | category | flops | bytes accessed | tf_op | source)
XLA Modules:
  0.0 533.8 jit_solution(3634788665941681921)
XLA Ops:
  9.9 7.1 %all-to-all-start = ((bf16[16,128,256]{2,1,0:T(8,128)(2,1)}), bf16[16,128,256]{2,1,0:T(8,128)(2,1)}, u32[]{:S(2)}, u32[]{:S(2)}) async-start(bf16[16,128,256]{2,1,0:T(8,128)(2,1)} %stack.2), calls=%async_computation | async-start | bytes 2097152 | tf_op jit(solution)/shard_map/all_to_all | solution.py:64
  17.0 18.0 %all-to-all-done = bf16[16,128,256]{2,1,0:T(8,128)(2,1)} async-done(((bf16[16,128,256]{2,1,0:T(8,128)(2,1)}), bf16[16,128,256]{2,1,0:T(8,128)(2,1)}, u32[]{:S(2)}, u32[]{:S(2)}) %all-to-all-start) | async-done | bytes 1048608 | tf_op jit(solution)/shard_map/all_to_all | solution.py:64
  35.1 2.4 broadcast_in_dim.111
  37.5 64.7 %while.26 = (s32[]{:T(128)}, f32[32,128,256]{2,1,0:T(8,128)}, s32[96]{0:T(128)S(1)}, s32[]{:T(128)}, bf16[96,128,128]{2,1,0:T(8,128)(2,1)}, /*index=5*/s32[96]{0...) while((s32[]{:T(128)}, f32[32,128,256]{2,1,0:T(8,128)}, ...), condition=%wide.region_2.3_spmd, body=%wide.region_0.2_spmd.sunk | while | flops 135529648 | bytes 14160559 | solution.py:39
  38.2 1.8 gather_fusion
  42.2 1.5 fusion.36
  43.8 4.4 scatter_fusion
  48.9 1.8 gather_fusion
  52.9 1.5 fusion.36
  54.5 4.4 scatter_fusion
  59.7 1.8 gather_fusion
  63.6 1.5 fusion.36
  65.2 4.5 scatter_fusion
  70.5 1.8 gather_fusion
  74.5 1.5 fusion.36
  76.1 4.5 scatter_fusion
  81.4 1.8 gather_fusion
  85.3 1.5 fusion.36
  87.0 4.5 scatter_fusion
  92.2 1.8 gather_fusion
  97.8 4.4 scatter_fusion
  102.2 3.8 convert_element_type.48
  106.1 135.9 %reduce-scatter.3.cloned.1.call-done = bf16[128,256]{1,0:T(8,128)(2,1)} async-done(((bf16[4096,256]{1,0:T(8,128)(2,1)}), bf16[128,256]{1,0:T(8,128)(2,1)}) %reduce-scatter.3.cloned.1.call-update) | async-done | bytes 65552 | tf_op jit(solution)/shard_map/reduce_scatter | solution.py:84
  242.0 1.7 multiply_convert_fusion.2
  244.7 132.9 %all-gather.2.cloned.1.call-done = bf16[4096,256]{1,0:T(8,128)(2,1)} async-done(((bf16[128,256]{1,0:T(8,128)(2,1)}), bf16[4096,256]{1,0:T(8,128)(2,1)}) %all-gather.2.cloned.1.call-update) | async-done | bytes 2097168 | tf_op jit(solution)/shard_map/all_gather | solution.py:94
  377.6 1.5 broadcast_in_dim.112
  379.1 53.5 %while.27 = (s32[]{:T(128)}, f32[16,128,256]{2,1,0:T(8,128)}, s32[96]{0:T(128)S(1)}, s32[]{:T(128)}, bf16[96,128,128]{2,1,0:T(8,128)(2,1)}, /*index=5*/s32[96]{0...) while((s32[]{:T(128)}, f32[16,128,256]{2,1,0:T(8,128)}, ...), condition=%wide.region_6.7_spmd, body=%wide.region_4.6_spmd.sunk | while | flops 135529648 | bytes 12063407 | solution.py:39
  379.9 2.2 gather_fusion.1
  382.1 1.5 fusion.39
  383.7 4.3 scatter_fusion.1
  388.8 2.2 gather_fusion.1
  391.0 1.5 fusion.39
  392.6 4.3 scatter_fusion.1
  397.6 2.2 gather_fusion.1
  399.9 1.5 fusion.39
  401.5 4.4 scatter_fusion.1
  406.6 2.2 gather_fusion.1
  408.8 1.5 fusion.39
  410.4 4.4 scatter_fusion.1
  415.5 2.2 gather_fusion.1
  417.7 1.5 fusion.39
  419.4 4.3 scatter_fusion.1
  424.4 2.2 gather_fusion.1
  426.7 1.5 fusion.39
  428.3 4.4 scatter_fusion.1
  432.6 2.7 convert_element_type.56
  435.4 90.3 %reduce-scatter.5.cloned.1.call-done = bf16[128,256]{1,0:T(8,128)(2,1)} async-done(((bf16[2048,256]{1,0:T(8,128)(2,1)}), bf16[128,256]{1,0:T(8,128)(2,1)}) %reduce-scatter.5.cloned.1.call-update) | async-done | bytes 65552 | tf_op jit(solution)/shard_map/reduce_scatter | solution.py:107
  525.7 1.6 multiply_convert_fusion
  (67 shorter events, 27.7 us)
Async XLA Ops:
  7.2 234.9 %copy-start = (bf16[256,256]{1,0:T(8,128)(2,1)S(1)}, bf16[256,256]{1,0:T(8,128)(2,1)}, u32[]{:S(2)}) copy-start(bf16[256,256]{1,0:T(8,128)(2,1)} %param.16) | copy-start | bytes 393220
  9.9 25.2 %all-to-all-start = ((bf16[16,128,256]{2,1,0:T(8,128)(2,1)}), bf16[16,128,256]{2,1,0:T(8,128)(2,1)}, u32[]{:S(2)}, u32[]{:S(2)}) async-start(bf16[16,128,256]{2,1,0:T(8,128)(2,1)} %stack.2), calls=%async_computation | async-start | bytes 2097152 | tf_op jit(solution)/shard_map/all_to_all | solution.py:64
  17.0 225.0 %reduce-scatter.3.cloned.1.call-start = ((), (), s32[]{:S(2)}) async-start(), calls=%async_computation.3 | async-start | bytes 2162688 | tf_op jit(solution)/shard_map/reduce_scatter | solution.py:84
  35.1 2.4 copy-start.1
  35.1 2.4 copy-start.2
  106.0 137.7 %copy-start.3 = (bf16[128,256]{1,0:T(8,128)(2,1)S(1)}, bf16[128,256]{1,0:T(8,128)(2,1)}, u32[]{:S(2)}) copy-start(bf16[128,256]{1,0:T(8,128)(2,1)} %param.17) | copy-start | bytes 196612
  106.1 271.5 %all-gather.2.cloned.1.call-start = ((), (), s32[]{:S(2)}) async-start(), calls=%async_computation.4 | async-start | bytes 2162688 | tf_op jit(solution)/shard_map/all_gather | solution.py:94
  244.6 281.1 %reduce-scatter.5.cloned.1.call-start = ((), (), s32[]{:S(2)}) async-start(), calls=%async_computation.5 | async-start | bytes 1114112 | tf_op jit(solution)/shard_map/reduce_scatter | solution.py:107
Sparse Core Ops, SparseCore 0:
  106.2 135.8 reduce-scatter.2
  244.9 132.6 all-gather.1
  435.5 90.1 reduce-scatter.4
